TPU v7x, 256 devices: a whole 4x4x8 slice. The times are simulated.
256 devices in a mesh: leaf: 32 (over x, z), row: 4 (over y), col: 2 (over core).
Axes of the slice: x: 4, y: 4, z: 8, core: 2. Of those that a mesh axis runs over, the one named last changes fastest.
Arguments:
- loads: float32 [3, 8192, 2, 256], P(None, ('leaf', 'row', 'col')), may hold values from -6 to 6
- pivot_root: float32 [2, 32, 4, 2, 32, 8192], P(None, None, 'row', 'col', None, 'leaf'), may hold values from -0.046875 to 0.046875
- pivot_mid: float32 [2, 16, 4, 2, 32, 8192], P(None, None, 'row', 'col', None, 'leaf'), may hold values from -0.0625 to 0.0625
- pivot_low: float32 [2, 8, 4, 2, 32, 8192], P(None, None, 'row', 'col', None, 'leaf'), may hold values from -0.09375 to 0.09375
- upper_mid: float32 [2, 16, 4, 2, 32, 8192], P(None, None, 'row', 'col', None, 'leaf'), may hold values from -0.0625 to 0.0625
- upper_low: float32 [2, 8, 4, 2, 32, 8192], P(None, None, 'row', 'col', None, 'leaf'), may hold values from -0.09375 to 0.09375
- lower_mid: float32 [2, 16, 4, 2, 32, 8192], P(None, None, 'row', 'col', None, 'leaf'), may hold values from -0.0625 to 0.0625
- lower_low: float32 [2, 8, 4, 2, 32, 8192], P(None, None, 'row', 'col', None, 'leaf'), may hold values from -0.09375 to 0.09375
- index_maps: int32 [2, 8192], P(None, ('leaf', 'row', 'col')), may hold values from 0 to 8191, as said below
Outputs:
- solution: float32 [3, 8192, 2, 256], P(None, ('leaf', 'row', 'col'))
Inputs may be any that keep to these rules, and one draw needn't show every extreme that they name: `index_maps`: row g of a child front lies in block d = g // 32; write d = i * 4 * 2 + c and let G be 32 / 2 for map 0 and 8 for map 1. Its parent row lies in the parent's block (i mod 2G) * 4 * 2 + c or ((i xor G) mod 2G) * 4 * 2 + c, and the parent rows of the rows of one block are distinct.
All inputs are finite; a program needn't handle non-finite values.
Results may differ from a plain program's by a relative error of at most 0.00013.
Values sent between devices are 32-bit elements; how exact they have to be, the bound alone decides.
No kernel may reach another device: no remote copies, remote signals or barrier semaphores. Data moves between devices by JAX's collectives and lax.ppermute only.
A program may use at most 64 MiB of HBM per device.

v0:
```python
import jax
import jax.numpy as jnp
from jax import lax
from jax.sharding import PartitionSpec as P


def swapped(shard, axis, bit):
    return lax.ppermute(shard, axis, [(i, i ^ 1 << bit) for i in range(lax.axis_size(axis))])


def conj_apply(matrix, vector):
    contract = (((0,), (0,)), ((), ()))

    def product(left, right):
        return lax.dot_general(
            left,
            right,
            contract,
            precision=lax.Precision.HIGHEST,
            preferred_element_type=jnp.float32,
        )

    real_part = product(matrix[0], vector[:, 0, :]) + product(matrix[1], vector[:, 1, :])
    imag_part = product(matrix[0], vector[:, 1, :]) - product(matrix[1], vector[:, 0, :])
    return jnp.stack([real_part, imag_part], axis=1)


def front_gather(block, bits):
    leaf_index = lax.axis_index("leaf")
    for bit_number in range(bits):
        other = swapped(block, "leaf", bit_number)
        upper = leaf_index >> bit_number & 1 == 1
        block = jnp.where(
            upper, jnp.concatenate([other, block], axis=0), jnp.concatenate([block, other], axis=0)
        )
    return block


def front_apply(matrix, vector, bits):
    local = matrix.reshape(2, -1, matrix.shape[-1])
    gathered = front_gather(vector, bits)
    return lax.psum_scatter(
        conj_apply(local, gathered), ("row", "col"), scatter_dimension=0, tiled=True
    )


def route_masks(index_block, group, rows):
    leaf_index = lax.axis_index("leaf")
    cell_index = lax.axis_index(("row", "col"))
    cells = lax.axis_size("row") * lax.axis_size("col")
    own_block = leaf_index % (2 * group) * cells + cell_index
    target = index_block // rows
    slot = index_block % rows
    picked = (slot[:, None] == jnp.arange(rows, dtype=jnp.int32)[None, :]).astype(jnp.float32)
    mine = picked * (target == own_block).astype(jnp.float32)[:, None]
    return (mine, picked - mine)


def send_upward(update, index_block, group):
    mine, theirs = route_masks(index_block, group, update.shape[0])
    to_self = jnp.einsum("tq,tcn->qcn", mine, update, precision=lax.Precision.HIGHEST)
    to_other = jnp.einsum("tq,tcn->qcn", theirs, update, precision=lax.Precision.HIGHEST)
    received = swapped(to_other, "leaf", group.bit_length() - 1)
    return to_self + received


def pull_down(parent, index_block, group):
    mine, theirs = route_masks(index_block, group, parent.shape[0])
    other = swapped(parent, "leaf", group.bit_length() - 1)
    own_part = jnp.einsum("tq,qcn->tcn", mine, parent, precision=lax.Precision.HIGHEST)
    other_part = jnp.einsum("tq,qcn->tcn", theirs, other, precision=lax.Precision.HIGHEST)
    return own_part + other_part


def solve_levels(
    loads, pivot_root, pivot_mid, pivot_low, upper_mid, upper_low, lower_mid, lower_low, index_maps
):
    leaf_count = lax.axis_size("leaf")
    bits = leaf_count.bit_length() - 1
    group_mid = leaf_count // 2
    group_low = leaf_count // 4
    inner_low = front_apply(pivot_low, loads[2], bits - 2)
    update_low = front_apply(upper_low, inner_low, bits - 2)
    right_mid = loads[1] - send_upward(update_low, index_maps[1], group_low)
    inner_mid = front_apply(pivot_mid, right_mid, bits - 1)
    update_mid = front_apply(upper_mid, inner_mid, bits - 1)
    right_root = loads[0] - send_upward(update_mid, index_maps[0], group_mid)
    inner_root = front_apply(pivot_root, right_root, bits)
    final_mid = inner_mid - front_apply(
        lower_mid, pull_down(inner_root, index_maps[0], group_mid), bits - 1
    )
    final_low = inner_low - front_apply(
        lower_low, pull_down(final_mid, index_maps[1], group_low), bits - 2
    )
    return jnp.stack([inner_root, final_mid, final_low])


def on_device(
    loads, pivot_root, pivot_mid, pivot_low, upper_mid, upper_low, lower_mid, lower_low, index_maps
):
    factors = (pivot_root, pivot_mid, pivot_low, upper_mid, upper_low, lower_mid, lower_low)
    return solve_levels(loads, *factors, index_maps)


def solution(mesh):
    in_specs = (
        P(None, ("leaf", "row", "col"), None, None),
        P(None, None, "row", "col", None, "leaf"),
        P(None, None, "row", "col", None, "leaf"),
        P(None, None, "row", "col", None, "leaf"),
        P(None, None, "row", "col", None, "leaf"),
        P(None, None, "row", "col", None, "leaf"),
        P(None, None, "row", "col", None, "leaf"),
        P(None, None, "row", "col", None, "leaf"),
        P(None, ("leaf", "row", "col")),
    )
    out_specs = P(None, ("leaf", "row", "col"), None, None)
    return jax.shard_map(
        on_device, mesh=mesh, in_specs=in_specs, out_specs=out_specs, check_vma=False
    )
```

profile of v0, /device:TPU:2, one launch (start us, length us, event | category | flops | bytes accessed | tf_op | source)
XLA Modules:
  0.0 815.4 jit_solution(5854912462377648872)
XLA Ops:
  9.5 2.3 collective-permute-done
  11.8 3.4 collective-permute-start.1
  15.2 5.3 collective-permute-done.1
  20.6 6.5 collective-permute-start.2
  28.1 10.3 %collective-permute-done.2 = f32[128,2,256]{2,0,1:T(8,128)S(1)} collective-permute-done((f32[128,2,256]{2,0,1:T(8,128)S(1)}, f32[128,2,256]{2,0,1:T(8,128)S(1)}, u32[]{:S(2)}, u32[]{:S(2)}) %collective-permute-start.2) | collective-permute-done | bytes 262176 | tf_op jit(solution)/shard_map/ppermute | solution.py:8
  43.3 64.0 %all-reduce.15.cloned.1.call-done = f32[256,2,256]{2,1,0:T(2,128)} async-done(((f32[256,2,256]{2,1,0:T(2,128)}), f32[256,2,256]{2,1,0:T(2,128)}) %all-reduce.15.cloned.1.call-update) | async-done | bytes 524304
  109.7 2.7 collective-permute-done.3
  112.4 3.3 collective-permute-start.4
  115.8 4.4 collective-permute-done.4
  120.1 10.7 %collective-permute-start.5 = (f32[128,2,256]{2,0,1:T(8,128)S(1)}, f32[128,2,256]{2,0,1:T(8,128)S(1)}, u32[]{:S(2)}, u32[]{:S(2)}) collective-permute-start(f32[128,2,256]{2,0,1:T(8,128)S(1)} %maximum_select_fusion.13), channel_id=1, source_target_pairs={{0,32},{8,40},{16,48},{24,56},{32,0},{40,8},{48,16},{56,24},{64,96... | collective-permute-start | bytes 786440 | tf_op jit(solution)/shard_map/ppermute | solution.py:8
  130.8 5.3 collective-permute-done.5
  139.8 65.7 %all-reduce.17.cloned.1.call-done = f32[256,2,256]{2,1,0:T(2,128)} async-done(((f32[256,2,256]{2,1,0:T(2,128)}), f32[256,2,256]{2,1,0:T(2,128)}) %all-reduce.17.cloned.1.call-update) | async-done | bytes 524304
  207.4 3.7 collective-permute-done.6
  213.1 3.6 collective-permute-done.7
  218.7 5.4 collective-permute-done.8
  224.1 10.9 %collective-permute-start.9 = (f32[128,2,256]{2,0,1:T(8,128)S(1)}, f32[128,2,256]{2,0,1:T(8,128)S(1)}, u32[]{:S(2)}, u32[]{:S(2)}) collective-permute-start(f32[128,2,256]{2,0,1:T(8,128)S(1)} %maximum_select_fusion.14), channel_id=1, source_target_pairs={{0,32},{8,40},{16,48},{24,56},{32,0},{40,8},{48,16},{56,24},{64,96... | collective-permute-start | bytes 786440 | tf_op jit(solution)/shard_map/ppermute | solution.py:8
  235.0 7.2 collective-permute-done.9
  243.1 8.5 %collective-permute-done.10 = f32[256,2,256]{2,0,1:T(8,128)S(1)} collective-permute-done((f32[256,2,256]{2,0,1:T(8,128)S(1)}, f32[256,2,256]{2,0,1:T(8,128)S(1)}, u32[]{:S(2)}, u32[]{:S(2)}) %collective-permute-start.10) | collective-permute-done | bytes 524320 | tf_op jit(solution)/shard_map/ppermute | solution.py:8
  257.0 65.6 %all-reduce.19.cloned.1.call-done = f32[256,2,256]{2,1,0:T(2,128)} async-done(((f32[256,2,256]{2,1,0:T(2,128)}), f32[256,2,256]{2,1,0:T(2,128)}) %all-reduce.19.cloned.1.call-update) | async-done | bytes 524304
  325.1 2.7 collective-permute-done.11
  327.8 3.3 collective-permute-start.12
  331.2 4.4 collective-permute-done.12
  335.5 10.7 %collective-permute-start.13 = (f32[128,2,256]{2,0,1:T(8,128)S(1)}, f32[128,2,256]{2,0,1:T(8,128)S(1)}, u32[]{:S(2)}, u32[]{:S(2)}) collective-permute-start(f32[128,2,256]{2,0,1:T(8,128)S(1)} %maximum_select_fusion.15), channel_id=1, source_target_pairs={{0,32},{8,40},{16,48},{24,56},{32,0},{40,8},{48,16},{56,24},{64,96... | collective-permute-start | bytes 786440 | tf_op jit(solution)/shard_map/ppermute | solution.py:8
  346.2 5.3 collective-permute-done.13
  352.3 8.5 %collective-permute-done.14 = f32[256,2,256]{2,0,1:T(8,128)S(1)} collective-permute-done((f32[256,2,256]{2,0,1:T(8,128)S(1)}, f32[256,2,256]{2,0,1:T(8,128)S(1)}, u32[]{:S(2)}, u32[]{:S(2)}) %collective-permute-start.14) | collective-permute-done | bytes 524320 | tf_op jit(solution)/shard_map/ppermute | solution.py:8
  366.1 70.0 %all-reduce.21.cloned.1.call-done = f32[256,2,256]{2,1,0:T(2,128)} async-done(((f32[256,2,256]{2,1,0:T(2,128)}), f32[256,2,256]{2,1,0:T(2,128)}) %all-reduce.21.cloned.1.call-update) | async-done | bytes 524304
  437.3 2.2 collective-permute-start.15
  439.5 3.7 collective-permute-done.15
  445.4 3.6 collective-permute-done.16
  451.0 5.4 collective-permute-done.17
  456.4 10.9 %collective-permute-start.18 = (f32[128,2,256]{2,0,1:T(8,128)S(1)}, f32[128,2,256]{2,0,1:T(8,128)S(1)}, u32[]{:S(2)}, u32[]{:S(2)}) collective-permute-start(f32[128,2,256]{2,0,1:T(8,128)S(1)} %maximum_select_fusion.16), channel_id=1, source_target_pairs={{0,32},{8,40},{16,48},{24,56},{32,0},{40,8},{48,16},{56,24},{64,96... | collective-permute-start | bytes 786440 | tf_op jit(solution)/shard_map/ppermute | solution.py:8
  467.3 7.2 collective-permute-done.18
  475.2 14.3 %collective-permute-done.19 = f32[256,2,256]{2,0,1:T(8,128)S(1)} collective-permute-done((f32[256,2,256]{2,0,1:T(8,128)S(1)}, f32[256,2,256]{2,0,1:T(8,128)S(1)}, u32[]{:S(2)}, u32[]{:S(2)}) %collective-permute-start.19) | collective-permute-done | bytes 524320 | tf_op jit(solution)/shard_map/ppermute | solution.py:8
  491.8 14.3 %collective-permute-done.20 = f32[512,2,256]{2,0,1:T(8,128)} collective-permute-done((f32[512,2,256]{2,0,1:T(8,128)S(1)}, f32[512,2,256]{2,0,1:T(8,128)}, u32[]{:S(2)}, u32[]{:S(2)}) %collective-permute-start.20) | collective-permute-done | bytes 1048608 | tf_op jit(solution)/shard_map/ppermute | solution.py:8
  516.6 69.4 %all-reduce.23.cloned.1.call-done = f32[256,2,256]{2,1,0:T(2,128)} async-done(((f32[256,2,256]{2,1,0:T(2,128)}), f32[256,2,256]{2,1,0:T(2,128)}) %all-reduce.23.cloned.1.call-update) | async-done | bytes 524304
  589.3 3.4 collective-permute-done.21
  594.7 3.6 collective-permute-done.22
  600.3 5.4 collective-permute-done.23
  605.7 11.2 %collective-permute-start.24 = (f32[128,2,256]{2,0,1:T(8,128)S(1)}, f32[128,2,256]{2,0,1:T(8,128)S(1)}, u32[]{:S(2)}, u32[]{:S(2)}) collective-permute-start(f32[128,2,256]{2,0,1:T(8,128)S(1)} %maximum_select_fusion.17), channel_id=1, source_target_pairs={{0,32},{8,40},{16,48},{24,56},{32,0},{40,8},{48,16},{56,24},{64,96... | collective-permute-start | bytes 786440 | tf_op jit(solution)/shard_map/ppermute | solution.py:8
  616.9 7.2 collective-permute-done.24
  624.9 8.5 %collective-permute-done.25 = f32[256,2,256]{2,0,1:T(8,128)S(1)} collective-permute-done((f32[256,2,256]{2,0,1:T(8,128)S(1)}, f32[256,2,256]{2,0,1:T(8,128)S(1)}, u32[]{:S(2)}, u32[]{:S(2)}) %collective-permute-start.25) | collective-permute-done | bytes 524320 | tf_op jit(solution)/shard_map/ppermute | solution.py:8
  638.7 65.7 %all-reduce.25.cloned.1.call-done = f32[256,2,256]{2,1,0:T(2,128)} async-done(((f32[256,2,256]{2,1,0:T(2,128)}), f32[256,2,256]{2,1,0:T(2,128)}) %all-reduce.25.cloned.1.call-update) | async-done | bytes 524304
  706.1 3.4 collective-permute-done.26
  711.5 3.6 collective-permute-done.27
  717.1 5.4 collective-permute-done.28
  722.5 10.9 %collective-permute-start.29 = (f32[128,2,256]{2,0,1:T(8,128)S(1)}, f32[128,2,256]{2,0,1:T(8,128)S(1)}, u32[]{:S(2)}, u32[]{:S(2)}) collective-permute-start(f32[128,2,256]{2,0,1:T(8,128)S(1)} %maximum_select_fusion.18), channel_id=1, source_target_pairs={{0,32},{8,40},{16,48},{24,56},{32,0},{40,8},{48,16},{56,24},{64,96... | collective-permute-start | bytes 786440 | tf_op jit(solution)/shard_map/ppermute | solution.py:8
  733.5 7.1 collective-permute-done.29
  744.2 62.2 %all-reduce.27.cloned.1.call-done = f32[256,2,256]{2,1,0:T(2,128)} async-done(((f32[256,2,256]{2,1,0:T(2,128)}), f32[256,2,256]{2,1,0:T(2,128)}) %all-reduce.27.cloned.1.call-update) | async-done | bytes 524304
  (151 shorter events, 77.7 us)
Async XLA Ops:
  6.5 100.7 %all-reduce.15.cloned.1.call-start = ((), (), s32[]{:S(2)}) async-start(), calls=%async_computation | async-start | bytes 1048576
  7.5 4.4 collective-permute-start
  11.8 8.7 %collective-permute-start.1 = (f32[64,2,256]{2,0,1:T(8,128)S(1)}, f32[64,2,256]{2,0,1:T(8,128)S(1)}, u32[]{:S(2)}, u32[]{:S(2)}) collective-permute-start(f32[64,2,256]{2,0,1:T(8,128)S(1)} %maximum_select_fusion.19), channel_id=1, source_target_pairs={{0,16},{8,24},{16,0},{24,8},{32,48},{40,56},{48,32},{56,40},{64,80... | collective-permute-start | bytes 393224 | tf_op jit(solution)/shard_map/ppermute | solution.py:8
  20.6 17.8 %collective-permute-start.2 = (f32[128,2,256]{2,0,1:T(8,128)S(1)}, f32[128,2,256]{2,0,1:T(8,128)S(1)}, u32[]{:S(2)}, u32[]{:S(2)}) collective-permute-start(f32[128,2,256]{2,0,1:T(8,128)S(1)} %maximum_select_fusion.12), channel_id=1, source_target_pairs={{0,32},{8,40},{16,48},{24,56},{32,0},{40,8},{48,16},{56,24},{64,96... | collective-permute-start | bytes 786440 | tf_op jit(solution)/shard_map/ppermute | solution.py:8
  40.2 1.8 copy-start.7
  40.8 90.0 %copy-start.4 = (f32[2,8,1,1,32,256]{5,4,3,2,1,0:T(8,128)S(1)}, f32[2,8,1,1,32,256]{5,4,3,2,1,0:T(8,128)}, u32[]{:S(2)}) copy-start(f32[2,8,1,1,32,256]{5,4,3,2,1,0:T(8,128)} %param.14) | copy-start | bytes 1572868
  42.0 163.6 %all-reduce.17.cloned.1.call-start = ((), (), s32[]{:S(2)}) async-start(), calls=%async_computation.1 | async-start | bytes 1048576
  108.1 4.4 collective-permute-start.3
  112.4 7.7 collective-permute-start.4
  120.1 16.0 %collective-permute-start.5 = (f32[128,2,256]{2,0,1:T(8,128)S(1)}, f32[128,2,256]{2,0,1:T(8,128)S(1)}, u32[]{:S(2)}, u32[]{:S(2)}) collective-permute-start(f32[128,2,256]{2,0,1:T(8,128)S(1)} %maximum_select_fusion.13), channel_id=1, source_target_pairs={{0,32},{8,40},{16,48},{24,56},{32,0},{40,8},{48,16},{56,24},{64,96... | collective-permute-start | bytes 786440 | tf_op jit(solution)/shard_map/ppermute | solution.py:8
  138.0 1.8 copy-start.6
  138.6 104.4 %copy-start.1 = (f32[2,16,1,1,32,256]{5,4,3,2,1,0:T(8,128)S(1)}, f32[2,16,1,1,32,256]{5,4,3,2,1,0:T(8,128)}, u32[]{:S(2)}) copy-start(f32[2,16,1,1,32,256]{5,4,3,2,1,0:T(8,128)} %param.11) | copy-start | bytes 3145732
  139.7 182.9 %all-reduce.19.cloned.1.call-start = ((), (), s32[]{:S(2)}) async-start(), calls=%async_computation.2 | async-start | bytes 1048576
  206.7 4.4 collective-permute-start.6
  211.4 5.3 collective-permute-start.7
  216.7 7.4 collective-permute-start.8
  224.1 18.1 %collective-permute-start.9 = (f32[128,2,256]{2,0,1:T(8,128)S(1)}, f32[128,2,256]{2,0,1:T(8,128)S(1)}, u32[]{:S(2)}, u32[]{:S(2)}) collective-permute-start(f32[128,2,256]{2,0,1:T(8,128)S(1)} %maximum_select_fusion.14), channel_id=1, source_target_pairs={{0,32},{8,40},{16,48},{24,56},{32,0},{40,8},{48,16},{56,24},{64,96... | collective-permute-start | bytes 786440 | tf_op jit(solution)/shard_map/ppermute | solution.py:8
  242.2 9.4 %collective-permute-start.10 = (f32[256,2,256]{2,0,1:T(8,128)S(1)}, f32[256,2,256]{2,0,1:T(8,128)S(1)}, u32[]{:S(2)}, u32[]{:S(2)}) collective-permute-start(f32[256,2,256]{2,0,1:T(8,128)S(1)} %maximum_select_fusion.7), channel_id=1, source_target_pairs={{0,64},{8,72},{16,80},{24,88},{32,96},{40,104},{48,112},{56,120},{... | collective-permute-start | bytes 1572872 | tf_op jit(solution)/shard_map/ppermute | solution.py:8
  255.9 96.3 %copy-start.2 = (f32[2,16,1,1,32,256]{5,4,3,2,1,0:T(8,128)S(1)}, f32[2,16,1,1,32,256]{5,4,3,2,1,0:T(8,128)}, u32[]{:S(2)}) copy-start(f32[2,16,1,1,32,256]{5,4,3,2,1,0:T(8,128)} %param.13) | copy-start | bytes 3145732
  256.9 179.2 %all-reduce.21.cloned.1.call-start = ((), (), s32[]{:S(2)}) async-start(), calls=%async_computation.3 | async-start | bytes 1048576
  323.5 4.4 collective-permute-start.11
  327.8 7.7 collective-permute-start.12
  335.5 16.0 %collective-permute-start.13 = (f32[128,2,256]{2,0,1:T(8,128)S(1)}, f32[128,2,256]{2,0,1:T(8,128)S(1)}, u32[]{:S(2)}, u32[]{:S(2)}) collective-permute-start(f32[128,2,256]{2,0,1:T(8,128)S(1)} %maximum_select_fusion.15), channel_id=1, source_target_pairs={{0,32},{8,40},{16,48},{24,56},{32,0},{40,8},{48,16},{56,24},{64,96... | collective-permute-start | bytes 786440 | tf_op jit(solution)/shard_map/ppermute | solution.py:8
  351.6 9.3 %collective-permute-start.14 = (f32[256,2,256]{2,0,1:T(8,128)S(1)}, f32[256,2,256]{2,0,1:T(8,128)S(1)}, u32[]{:S(2)}, u32[]{:S(2)}) collective-permute-start(f32[256,2,256]{2,0,1:T(8,128)S(1)} %maximum_select_fusion.8), channel_id=1, source_target_pairs={{0,64},{8,72},{16,80},{24,88},{32,96},{40,104},{48,112},{56,120},{... | collective-permute-start | bytes 1572872 | tf_op jit(solution)/shard_map/ppermute | solution.py:8
  366.1 220.0 %all-reduce.23.cloned.1.call-start = ((), (), s32[]{:S(2)}) async-start(), calls=%async_computation.4 | async-start | bytes 1048576
  437.3 5.9 collective-permute-start.15
  443.2 48.5 %copy-start = (f32[2,32,1,1,32,256]{5,4,3,2,1,0:T(8,128)S(1)}, f32[2,32,1,1,32,256]{5,4,3,2,1,0:T(8,128)}, u32[]{:S(2)}) copy-start(f32[2,32,1,1,32,256]{5,4,3,2,1,0:T(8,128)} %param.10) | copy-start | bytes 6291460
  443.5 5.5 collective-permute-start.16
  449.0 7.4 collective-permute-start.17
  456.4 18.1 %collective-permute-start.18 = (f32[128,2,256]{2,0,1:T(8,128)S(1)}, f32[128,2,256]{2,0,1:T(8,128)S(1)}, u32[]{:S(2)}, u32[]{:S(2)}) collective-permute-start(f32[128,2,256]{2,0,1:T(8,128)S(1)} %maximum_select_fusion.16), channel_id=1, source_target_pairs={{0,32},{8,40},{16,48},{24,56},{32,0},{40,8},{48,16},{56,24},{64,96... | collective-permute-start | bytes 786440 | tf_op jit(solution)/shard_map/ppermute | solution.py:8
  474.5 14.9 %collective-permute-start.19 = (f32[256,2,256]{2,0,1:T(8,128)S(1)}, f32[256,2,256]{2,0,1:T(8,128)S(1)}, u32[]{:S(2)}, u32[]{:S(2)}) collective-permute-start(f32[256,2,256]{2,0,1:T(8,128)S(1)} %maximum_select_fusion.9), channel_id=1, source_target_pairs={{0,64},{8,72},{16,80},{24,88},{32,96},{40,104},{48,112},{56,120},{... | collective-permute-start | bytes 1572872 | tf_op jit(solution)/shard_map/ppermute | solution.py:8
  489.6 16.5 %collective-permute-start.20 = (f32[512,2,256]{2,0,1:T(8,128)S(1)}, f32[512,2,256]{2,0,1:T(8,128)}, u32[]{:S(2)}, u32[]{:S(2)}) collective-permute-start(f32[512,2,256]{2,0,1:T(8,128)S(1)} %maximum_select_fusion.3), channel_id=1, source_target_pairs={{0,128},{8,136},{16,144},{24,152},{32,160},{40,168},{48,176},{56,1... | collective-permute-start | bytes 3145736 | tf_op jit(solution)/shard_map/ppermute | solution.py:8
  515.5 109.3 %copy-start.3 = (f32[2,16,1,1,32,256]{5,4,3,2,1,0:T(8,128)S(1)}, f32[2,16,1,1,32,256]{5,4,3,2,1,0:T(8,128)}, u32[]{:S(2)}) copy-start(f32[2,16,1,1,32,256]{5,4,3,2,1,0:T(8,128)} %param.15) | copy-start | bytes 3145732
  516.6 187.8 %all-reduce.25.cloned.1.call-start = ((), (), s32[]{:S(2)}) async-start(), calls=%async_computation.5 | async-start | bytes 1048576
  586.9 5.9 collective-permute-start.21
  593.0 5.3 collective-permute-start.22
  598.3 7.4 collective-permute-start.23
  605.7 18.4 %collective-permute-start.24 = (f32[128,2,256]{2,0,1:T(8,128)S(1)}, f32[128,2,256]{2,0,1:T(8,128)S(1)}, u32[]{:S(2)}, u32[]{:S(2)}) collective-permute-start(f32[128,2,256]{2,0,1:T(8,128)S(1)} %maximum_select_fusion.17), channel_id=1, source_target_pairs={{0,32},{8,40},{16,48},{24,56},{32,0},{40,8},{48,16},{56,24},{64,96... | collective-permute-start | bytes 786440 | tf_op jit(solution)/shard_map/ppermute | solution.py:8
  624.1 9.3 %collective-permute-start.25 = (f32[256,2,256]{2,0,1:T(8,128)S(1)}, f32[256,2,256]{2,0,1:T(8,128)S(1)}, u32[]{:S(2)}, u32[]{:S(2)}) collective-permute-start(f32[256,2,256]{2,0,1:T(8,128)S(1)} %maximum_select_fusion.10), channel_id=1, source_target_pairs={{0,64},{8,72},{16,80},{24,88},{32,96},{40,104},{48,112},{56,120},{... | collective-permute-start | bytes 1572872 | tf_op jit(solution)/shard_map/ppermute | solution.py:8
  637.5 95.9 %copy-start.5 = (f32[2,8,1,1,32,256]{5,4,3,2,1,0:T(8,128)S(1)}, f32[2,8,1,1,32,256]{5,4,3,2,1,0:T(8,128)}, u32[]{:S(2)}) copy-start(f32[2,8,1,1,32,256]{5,4,3,2,1,0:T(8,128)} %param.16) | copy-start | bytes 1572868
  638.6 167.8 %all-reduce.27.cloned.1.call-start = ((), (), s32[]{:S(2)}) async-start(), calls=%async_computation.6 | async-start | bytes 1048576
  705.2 4.4 collective-permute-start.26
  709.8 5.2 collective-permute-start.27
  715.1 7.4 collective-permute-start.28
  722.5 18.1 %collective-permute-start.29 = (f32[128,2,256]{2,0,1:T(8,128)S(1)}, f32[128,2,256]{2,0,1:T(8,128)S(1)}, u32[]{:S(2)}, u32[]{:S(2)}) collective-permute-start(f32[128,2,256]{2,0,1:T(8,128)S(1)} %maximum_select_fusion.18), channel_id=1, source_target_pairs={{0,32},{8,40},{16,48},{24,56},{32,0},{40,8},{48,16},{56,24},{64,96... | collective-permute-start | bytes 786440 | tf_op jit(solution)/shard_map/ppermute | solution.py:8
Sparse Core Ops, SparseCore 0:
  42.1 65.0 all-reduce.14
  139.8 65.7 all-reduce.16
  257.1 65.5 all-reduce.18
  366.2 69.9 all-reduce.20
  516.7 69.3 all-reduce.22
  638.8 65.5 all-reduce.24
  744.3 62.0 all-reduce.26
where the time goes:
time: 824 us; the launch traced here: 815 us
  waiting for transfers between devices  638 us (77%)
  starting transfers between devices  113 us (14%)
  matrix products  29.1 us (4%)
  local copies, waits for them, and re-layouts  17 us (2%)
  between operations  15.3 us (2%)
    unnamed x14, waiting for transfers between devices  463 us
    ppermute x30, waiting for transfers between devices, swapped(): lax.ppermute(shard, axis, [(i, i ^ 1 << bit) for i in range(lax.axis_size...  176 us
    ppermute x30, starting transfers between devices, swapped(): lax.ppermute(shard, axis, [(i, i ^ 1 << bit) for i in range(lax.axis_size...  112 us
    dot_general x28, matrix products, product(): lax.dot_general(left, right, contract, precision=lax.Precision.HIGHEST, p...  26.7 us
  transfers between devices with their start and end apart: 37, of which 37 were waited for; matrix products, arithmetic and copies ran while one was open for 0% of the time, Pallas kernels for 0%

commit v1 on v0

v1 whole, which is shorter than its diff:
```python
import jax
import jax.numpy as jnp
from jax import lax
from jax.sharding import PartitionSpec as P

NEAR = 8


def product(left, right):
    contract = (((0,), (0,)), ((), ()))
    return lax.dot_general(
        left,
        right,
        contract,
        precision=lax.Precision.HIGH,
        preferred_element_type=jnp.float32,
    )


def swapped(shard, bit):
    return lax.ppermute(shard, "leaf", [(i, i ^ 1 << bit) for i in range(lax.axis_size("leaf"))])


def shifted(shard, far):
    count = lax.axis_size("leaf")
    return lax.ppermute(shard, "leaf", [(i, (i - far * NEAR) % count) for i in range(count)])


def near_gather(block):
    count = lax.axis_size("leaf")
    groups = [list(range(start, start + NEAR)) for start in range(0, count, NEAR)]
    spread = jnp.broadcast_to(block[None], (NEAR,) + block.shape)
    gathered = lax.all_to_all(spread, "leaf", 0, 0, axis_index_groups=groups)
    return gathered.reshape(NEAR * block.shape[0], block.shape[1])


def conj_apply(matrix, vector):
    half = vector.shape[1] // 2
    turned = jnp.concatenate([vector[:, half:], -vector[:, :half]], axis=1)
    return product(matrix.reshape(-1, matrix.shape[-1]), jnp.concatenate([vector, turned], axis=0))


def cell_scatter(partial):
    row, col = lax.axis_index("row"), lax.axis_index("col")
    rows = lax.axis_size("row")
    parts = partial.reshape(rows, 2, -1, partial.shape[-1])
    theirs = lax.dynamic_index_in_dim(parts, 1 - col, 1, keepdims=False)
    mine = lax.dynamic_index_in_dim(parts, col, 1, keepdims=False)
    summed = mine + lax.ppermute(theirs, "col", [(0, 1), (1, 0)])
    total = lax.dynamic_index_in_dim(summed, row, 0, keepdims=False)
    for step in (2, 1, 3):
        piece = lax.dynamic_index_in_dim(summed, (row + step) % rows, 0, keepdims=False)
        total = total + lax.ppermute(piece, "row", [(i, (i + step) % rows) for i in range(rows)])
    return total


def front_apply(matrix, block, wide):
    local = matrix.reshape(2, wide, -1, matrix.shape[-1])
    gathered = near_gather(block)
    far = lax.axis_index("leaf") // NEAR
    pieces = [(far % wide, gathered)]
    if wide == 2:
        pieces.append(((far + 1) % 2, swapped(gathered, 3)))
    elif wide == 4:
        pieces += [((far + step) % 4, shifted(gathered, step)) for step in (2, 1, 3)]
    partial = None
    for at, vector in pieces:
        term = conj_apply(lax.dynamic_index_in_dim(local, at, 1, keepdims=False), vector)
        partial = term if partial is None else partial + term
    return cell_scatter(partial)


def route_masks(index_block, group, rows):
    leaf_index = lax.axis_index("leaf")
    cell_index = lax.axis_index(("row", "col"))
    cells = lax.axis_size("row") * lax.axis_size("col")
    own_block = leaf_index % (2 * group) * cells + cell_index
    target = index_block // rows
    slot = index_block % rows
    picked = (slot[:, None] == jnp.arange(rows, dtype=jnp.int32)[None, :]).astype(jnp.float32)
    mine = picked * (target == own_block).astype(jnp.float32)[:, None]
    return (mine, picked - mine)


def send_upward(update, masks, group):
    mine, theirs = masks
    to_other = product(theirs, update)
    received = swapped(to_other, group.bit_length() - 1)
    return product(mine, update) + received


def pull_down(parent, masks, group):
    mine, theirs = masks
    other = swapped(parent, group.bit_length() - 1)
    return product(mine.T, parent) + product(theirs.T, other)


def on_device(
    loads, pivot_root, pivot_mid, pivot_low, upper_mid, upper_low, lower_mid, lower_low, index_maps
):
    group_mid = lax.axis_size("leaf") // 2
    group_low = lax.axis_size("leaf") // 4
    levels, rows = loads.shape[:2]
    flat = loads.reshape(levels, rows, -1)
    up_mid = route_masks(index_maps[0], group_mid, rows)
    up_low = route_masks(index_maps[1], group_low, rows)
    inner_low = front_apply(pivot_low, flat[2], 1)
    update_low = front_apply(upper_low, inner_low, 1)
    right_mid = flat[1] - send_upward(update_low, up_low, group_low)
    inner_mid = front_apply(pivot_mid, right_mid, 2)
    update_mid = front_apply(upper_mid, inner_mid, 2)
    right_root = flat[0] - send_upward(update_mid, up_mid, group_mid)
    inner_root = front_apply(pivot_root, right_root, 4)
    final_mid = inner_mid - front_apply(lower_mid, pull_down(inner_root, up_mid, group_mid), 2)
    final_low = inner_low - front_apply(lower_low, pull_down(final_mid, up_low, group_low), 1)
    return jnp.stack([inner_root, final_mid, final_low]).reshape(loads.shape)


def solution(mesh):
    matrix = P(None, None, "row", "col", None, "leaf")
    vectors = P(None, ("leaf", "row", "col"), None, None)
    in_specs = (vectors,) + (matrix,) * 7 + (P(None, ("leaf", "row", "col")),)
    return jax.shard_map(
        on_device, mesh=mesh, in_specs=in_specs, out_specs=vectors, check_vma=False
    )
```

time: 824 us -> 302 us (0.37)
  waiting for transfers between devices: 638 us -> 133 us
  blocking collectives: 0 us -> 75.7 us
  starting transfers between devices: 113 us -> 72.7 us
  matrix products: 29.1 us -> 10.3 us
  between operations: 15.3 us -> 0.92 us
  local copies, waits for them, and re-layouts: 17 us -> 6.22 us
    unnamed x14 -> x0, waiting for transfers between devices: 463 us -> none
    ppermute x30 -> x38, waiting for transfers between devices: 176 us -> 84.8 us  [the longest x7 41.3 us: swapped(): lax.ppermute(shard, 'leaf', [(i, i ^ 1 << bit) for i in range(lax.axis_si...]
    all_to_all x0 -> x4, blocking collectives: none -> 75.7 us  [near_gather(): gathered = lax.all_to_all(spread, 'leaf', 0, 0, axis_index_groups=groups)]
    ppermute x30 -> x38, starting transfers between devices: 112 us -> 57.3 us  [the longest x21 44.2 us: cell_scatter(): lax.ppermute(piece, 'row', [(i, (i + step) % rows) for i in range(rows)])]
    all_to_all x0 -> x3, waiting for transfers between devices: none -> 48.5 us  [near_gather(): gathered = lax.all_to_all(spread, 'leaf', 0, 0, axis_index_groups=groups)]
    dot_general x36 -> x21, matrix products: 29.1 us -> 10.3 us  [product(): lax.dot_general(left, right, contract, precision=lax.Precision.HIGH, pref...]
    all_to_all x0 -> x3, starting transfers between devices: none -> 15.4 us  [near_gather(): gathered = lax.all_to_all(spread, 'leaf', 0, 0, axis_index_groups=groups)]
  transfers between devices with their start and end apart: 37 -> 41, of which waited for: 37 -> 29; matrix products, arithmetic and copies ran while one was open for 0% -> 2% of each run, Pallas kernels for 0% -> 0%
where the time goes in v1:
time: 302 us; the launch traced here: 301 us
  waiting for transfers between devices  133 us (44%)
  blocking collectives  75.7 us (25%)
  starting transfers between devices  72.7 us (24%)
  matrix products  10.3 us (3%)
  local copies, waits for them, and re-layouts  6.22 us (2%)
    all_to_all x4, blocking collectives, near_gather(): gathered = lax.all_to_all(spread, 'leaf', 0, 0, axis_index_groups=groups)  75.7 us
    all_to_all x3, waiting for transfers between devices, near_gather(): gathered = lax.all_to_all(spread, 'leaf', 0, 0, axis_index_groups=groups)  48.5 us
    ppermute x21, starting transfers between devices, cell_scatter(): lax.ppermute(piece, 'row', [(i, (i + step) % rows) for i in range(rows)])  44.2 us
    ppermute x7, waiting for transfers between devices, swapped(): lax.ppermute(shard, 'leaf', [(i, i ^ 1 << bit) for i in range(lax.axis_si...  41.3 us
    ppermute x3, waiting for transfers between devices, shifted(): lax.ppermute(shard, 'leaf', [(i, (i - far * NEAR) % count) for i in range...  16.5 us
    ppermute x21, waiting for transfers between devices, cell_scatter(): lax.ppermute(piece, 'row', [(i, (i + step) % rows) for i in range(rows)])  16.4 us
    all_to_all x3, starting transfers between devices, near_gather(): gathered = lax.all_to_all(spread, 'leaf', 0, 0, axis_index_groups=groups)  15.4 us
    ppermute x7, waiting for transfers between devices, cell_scatter(): summed = mine + lax.ppermute(theirs, 'col', [(0, 1), (1, 0)])  10.5 us
  transfers between devices with their start and end apart: 41, of which 29 were waited for; matrix products, arithmetic and copies ran while one was open for 2% of the time, Pallas kernels for 0%

profile of v1, /device:TPU:2, one launch (start us, length us, event | category | flops | bytes accessed | tf_op | source)
XLA Modules:
  0.0 300.8 jit_solution(11340291992978880174)
XLA Ops:
  1.9 8.5 %all-to-all-start = ((f32[8,32,512]{2,1,0:T(8,128)}), f32[8,32,512]{2,1,0:T(8,128)S(1)}, u32[]{:S(2)}, u32[]{:S(2)}) async-start(f32[8,32,512]{2,1,0:T(8,128)} %broadcast_in_dim.17), calls=%async_computation | async-start | bytes 1048576 | tf_op jit(solution)/shard_map/all_to_all | solution.py:33
  10.3 17.5 %all-to-all-done = f32[8,32,512]{2,1,0:T(8,128)S(1)} async-done(((f32[8,32,512]{2,1,0:T(8,128)}), f32[8,32,512]{2,1,0:T(8,128)S(1)}, u32[]{:S(2)}, u32[]{:S(2)}) %all-to-all-start) | async-done | bytes 524320 | tf_op jit(solution)/shard_map/all_to_all | solution.py:33
  30.2 3.3 %collective-permute-start.1 = (f32[32,512]{1,0:T(8,128)S(1)}, f32[32,512]{1,0:T(8,128)S(1)}, u32[]{:S(2)}, u32[]{:S(2)}) collective-permute-start(f32[32,512]{1,0:T(8,128)S(1)} %get-tuple-element.63), channel_id=1, source_target_pairs={{0,4},{2,6},{4,0},{6,2},{1,5},{3,7},{5,1},{7,3},{8,12},{10,14},{12... | collective-permute-start | bytes 196616 | tf_op jit(solution)/shard_map/ppermute | solution.py:53
  34.2 2.6 collective-permute-start.3
  36.8 2.2 collective-permute-done.2
  39.1 19.1 %all_to_all.35 = f32[8,32,512]{2,1,0:T(8,128)S(1)} all-to-all(f32[8,32,512]{2,1,0:T(8,128)S(1)} %broadcast_in_dim.18), channel_id=1, replica_groups={{0,8,16,24,32,40,48,56},{64,72,80,88,96,104,112,120},{128,136,144,152,1..., dimensions={0} | all-to-all | bytes 1048576 | tf_op jit(solution)/shard_map/all_to_all | solution.py:33
  60.6 1.8 collective-permute-start.5
  62.4 2.1 collective-permute-start.6
  69.7 3.7 %collective-permute-done.8 = f32[32,512]{1,0:T(8,128)S(1)} collective-permute-done((f32[32,512]{1,0:T(8,128)S(1)}, f32[32,512]{1,0:T(8,128)S(1)}, u32[]{:S(2)}, u32[]{:S(2)}) %collective-permute-start.8) | collective-permute-done | bytes 65568 | tf_op jit(solution)/shard_map/ppermute | solution.py:21
  74.6 3.5 %all-to-all-start.2 = ((f32[8,32,512]{2,1,0:T(8,128)}), f32[8,32,512]{2,1,0:T(8,128)S(1)}, u32[]{:S(2)}, u32[]{:S(2)}) async-start(f32[8,32,512]{2,1,0:T(8,128)} %broadcast_in_dim.19), calls=%async_computation.2 | async-start | bytes 1048576 | tf_op jit(solution)/shard_map/all_to_all | solution.py:33
  78.1 15.4 %all-to-all-done.2 = f32[8,32,512]{2,1,0:T(8,128)S(1)} async-done(((f32[8,32,512]{2,1,0:T(8,128)}), f32[8,32,512]{2,1,0:T(8,128)S(1)}, u32[]{:S(2)}, u32[]{:S(2)}) %all-to-all-start.2) | async-done | bytes 524320 | tf_op jit(solution)/shard_map/all_to_all | solution.py:33
  94.9 9.1 %collective-permute-done.9 = f32[256,512]{1,0:T(8,128)S(1)} collective-permute-done((f32[256,512]{1,0:T(8,128)S(1)}, f32[256,512]{1,0:T(8,128)S(1)}, u32[]{:S(2)}, u32[]{:S(2)}) %collective-permute-start.9) | collective-permute-done | bytes 524320 | tf_op jit(solution)/shard_map/ppermute | solution.py:21
  106.4 2.4 collective-permute-start.11
  109.7 2.4 collective-permute-start.13
  112.3 2.1 collective-permute-done.12
  114.4 19.4 %all_to_all.36 = f32[8,32,512]{2,1,0:T(8,128)S(1)} all-to-all(f32[8,32,512]{2,1,0:T(8,128)S(1)} %broadcast_in_dim.20), channel_id=1, replica_groups={{0,8,16,24,32,40,48,56},{64,72,80,88,96,104,112,120},{128,136,144,152,1..., dimensions={0} | all-to-all | bytes 1048576 | tf_op jit(solution)/shard_map/all_to_all | solution.py:33
  135.2 9.1 %collective-permute-done.14 = f32[256,512]{1,0:T(8,128)S(1)} collective-permute-done((f32[256,512]{1,0:T(8,128)S(1)}, f32[256,512]{1,0:T(8,128)S(1)}, u32[]{:S(2)}, u32[]{:S(2)}) %collective-permute-start.14) | collective-permute-done | bytes 524320 | tf_op jit(solution)/shard_map/ppermute | solution.py:21
  146.7 2.3 collective-permute-start.16
  149.0 2.2 collective-permute-start.17
  151.2 2.6 collective-permute-start.18
  153.8 2.2 collective-permute-done.17
  156.3 2.4 collective-permute-start.19
  158.7 3.5 %collective-permute-done.19 = f32[32,512]{1,0:T(8,128)S(1)} collective-permute-done((f32[32,512]{1,0:T(8,128)S(1)}, f32[32,512]{1,0:T(8,128)S(1)}, u32[]{:S(2)}, u32[]{:S(2)}) %collective-permute-start.19) | collective-permute-done | bytes 65568 | tf_op jit(solution)/shard_map/ppermute | solution.py:21
  163.4 3.5 %all-to-all-start.4 = ((f32[8,32,512]{2,1,0:T(8,128)}), f32[8,32,512]{2,1,0:T(8,128)S(1)}, u32[]{:S(2)}, u32[]{:S(2)}) async-start(f32[8,32,512]{2,1,0:T(8,128)} %broadcast_in_dim.21), calls=%async_computation.4 | async-start | bytes 1048576 | tf_op jit(solution)/shard_map/all_to_all | solution.py:33
  167.0 15.6 %all-to-all-done.4 = f32[8,32,512]{2,1,0:T(8,128)S(1)} async-done(((f32[8,32,512]{2,1,0:T(8,128)}), f32[8,32,512]{2,1,0:T(8,128)S(1)}, u32[]{:S(2)}, u32[]{:S(2)}) %all-to-all-start.4) | async-done | bytes 524320 | tf_op jit(solution)/shard_map/all_to_all | solution.py:33
  182.6 2.3 collective-permute-start.20
  184.9 1.7 constant_dynamic-slice_fusion.3
  186.7 2.1 collective-permute-start.21
  189.4 9.5 %collective-permute-done.20 = f32[256,512]{1,0:T(8,128)S(1)} collective-permute-done((f32[256,512]{1,0:T(8,128)S(1)}, f32[256,512]{1,0:T(8,128)S(1)}, u32[]{:S(2)}, u32[]{:S(2)}) %collective-permute-start.20) | collective-permute-done | bytes 524320 | tf_op jit(solution)/shard_map/ppermute | solution.py:26
  199.0 7.0 %collective-permute-done.22 = f32[256,512]{1,0:T(8,128)S(1)} collective-permute-done((f32[256,512]{1,0:T(8,128)S(1)}, f32[256,512]{1,0:T(8,128)S(1)}, u32[]{:S(2)}, u32[]{:S(2)}) %collective-permute-start.22) | collective-permute-done | bytes 524320 | tf_op jit(solution)/shard_map/ppermute | solution.py:26
  209.8 2.8 collective-permute-start.24
  212.6 1.9 collective-permute-start.25
  214.5 2.6 collective-permute-start.26
  217.1 2.2 collective-permute-done.25
  219.3 2.3 collective-permute-start.27
  221.6 3.6 %collective-permute-done.27 = f32[32,512]{1,0:T(8,128)S(1)} collective-permute-done((f32[32,512]{1,0:T(8,128)S(1)}, f32[32,512]{1,0:T(8,128)S(1)}, u32[]{:S(2)}, u32[]{:S(2)}) %collective-permute-start.27) | collective-permute-done | bytes 65568 | tf_op jit(solution)/shard_map/ppermute | solution.py:21
  225.7 18.2 %all_to_all.37 = f32[8,32,512]{2,1,0:T(8,128)S(1)} all-to-all(f32[8,32,512]{2,1,0:T(8,128)S(1)} %broadcast_in_dim.22), channel_id=1, replica_groups={{0,8,16,24,32,40,48,56},{64,72,80,88,96,104,112,120},{128,136,144,152,1..., dimensions={0} | all-to-all | bytes 1048576 | tf_op jit(solution)/shard_map/all_to_all | solution.py:33
  245.3 8.8 %collective-permute-done.28 = f32[256,512]{1,0:T(8,128)S(1)} collective-permute-done((f32[256,512]{1,0:T(8,128)S(1)}, f32[256,512]{1,0:T(8,128)S(1)}, u32[]{:S(2)}, u32[]{:S(2)}) %collective-permute-start.28) | collective-permute-done | bytes 524320 | tf_op jit(solution)/shard_map/ppermute | solution.py:21
  256.5 2.1 collective-permute-start.30
  258.7 1.6 collective-permute-start.31
  260.3 2.6 collective-permute-start.32
  262.8 2.2 collective-permute-done.31
  265.9 3.5 %collective-permute-done.33 = f32[32,512]{1,0:T(8,128)S(1)} collective-permute-done((f32[32,512]{1,0:T(8,128)S(1)}, f32[32,512]{1,0:T(8,128)S(1)}, u32[]{:S(2)}, u32[]{:S(2)}) %collective-permute-start.33) | collective-permute-done | bytes 65568 | tf_op jit(solution)/shard_map/ppermute | solution.py:21
  270.0 19.0 %all_to_all.38 = f32[8,32,512]{2,1,0:T(8,128)S(1)} all-to-all(f32[8,32,512]{2,1,0:T(8,128)S(1)} %broadcast_in_dim.23), channel_id=1, replica_groups={{0,8,16,24,32,40,48,56},{64,72,80,88,96,104,112,120},{128,136,144,152,1..., dimensions={0} | all-to-all | bytes 1048576 | tf_op jit(solution)/shard_map/all_to_all | solution.py:33
  289.8 1.5 collective-permute-done.34
  291.4 3.1 %collective-permute-start.35 = (f32[32,512]{1,0:T(8,128)S(1)}, f32[32,512]{1,0:T(8,128)S(1)}, u32[]{:S(2)}, u32[]{:S(2)}) collective-permute-start(f32[32,512]{1,0:T(8,128)S(1)} %get-tuple-element.45), channel_id=1, source_target_pairs={{0,4},{2,6},{4,0},{6,2},{1,5},{3,7},{5,1},{7,3},{8,12},{10,14},{12... | collective-permute-start | bytes 196616 | tf_op jit(solution)/shard_map/ppermute | solution.py:53
  295.3 2.4 collective-permute-start.37
  297.8 2.1 collective-permute-done.36
  (134 shorter events, 36.3 us)
Async XLA Ops:
  0.0 27.9 %copy-start = (f32[2,8,1,1,32,256]{5,4,3,2,1,0:T(8,128)S(1)}, f32[2,8,1,1,32,256]{5,4,3,2,1,0:T(8,128)}, u32[]{:S(2)}) copy-start(f32[2,8,1,1,32,256]{5,4,3,2,1,0:T(8,128)} %param.12) | copy-start | bytes 1572868
  1.9 26.0 %all-to-all-start = ((f32[8,32,512]{2,1,0:T(8,128)}), f32[8,32,512]{2,1,0:T(8,128)S(1)}, u32[]{:S(2)}, u32[]{:S(2)}) async-start(f32[8,32,512]{2,1,0:T(8,128)} %broadcast_in_dim.17), calls=%async_computation | async-start | bytes 1048576 | tf_op jit(solution)/shard_map/all_to_all | solution.py:33
  28.5 1.6 collective-permute-start
  28.7 29.5 %copy-start.4 = (f32[2,8,1,1,32,256]{5,4,3,2,1,0:T(8,128)S(1)}, f32[2,8,1,1,32,256]{5,4,3,2,1,0:T(8,128)}, u32[]{:S(2)}) copy-start(f32[2,8,1,1,32,256]{5,4,3,2,1,0:T(8,128)} %param.14) | copy-start | bytes 1572868
  30.2 6.5 %collective-permute-start.1 = (f32[32,512]{1,0:T(8,128)S(1)}, f32[32,512]{1,0:T(8,128)S(1)}, u32[]{:S(2)}, u32[]{:S(2)}) collective-permute-start(f32[32,512]{1,0:T(8,128)S(1)} %get-tuple-element.63), channel_id=1, source_target_pairs={{0,4},{2,6},{4,0},{6,2},{1,5},{3,7},{5,1},{7,3},{8,12},{10,14},{12... | collective-permute-start | bytes 196616 | tf_op jit(solution)/shard_map/ppermute | solution.py:53
  33.5 5.5 %collective-permute-start.2 = (f32[32,512]{1,0:T(8,128)S(1)}, f32[32,512]{1,0:T(8,128)S(1)}, u32[]{:S(2)}, u32[]{:S(2)}) collective-permute-start(f32[32,512]{1,0:T(8,128)S(1)} %get-tuple-element.65), channel_id=1, source_target_pairs={{0,2},{2,4},{4,6},{6,0},{1,3},{3,5},{5,7},{7,1},{8,10},{10,12},{12... | collective-permute-start | bytes 196616 | tf_op jit(solution)/shard_map/ppermute | solution.py:53
  34.2 4.8 %collective-permute-start.3 = (f32[32,512]{1,0:T(8,128)S(1)}, f32[32,512]{1,0:T(8,128)S(1)}, u32[]{:S(2)}, u32[]{:S(2)}) collective-permute-start(f32[32,512]{1,0:T(8,128)S(1)} %get-tuple-element.64), channel_id=1, source_target_pairs={{0,6},{2,0},{4,2},{6,4},{1,7},{3,1},{5,3},{7,5},{8,14},{10,8},{12,... | collective-permute-start | bytes 196616 | tf_op jit(solution)/shard_map/ppermute | solution.py:53
  58.1 0.9 copy-start.6
  58.8 35.3 %copy-start.3 = (f32[2,16,1,1,32,256]{5,4,3,2,1,0:T(8,128)S(1)}, f32[2,16,1,1,32,256]{5,4,3,2,1,0:T(8,128)}, u32[]{:S(2)}) copy-start(f32[2,16,1,1,32,256]{5,4,3,2,1,0:T(8,128)} %param.11) | copy-start | bytes 3145732
  58.9 1.6 collective-permute-start.4
  60.6 6.0 %collective-permute-start.5 = (f32[32,512]{1,0:T(8,128)S(1)}, f32[32,512]{1,0:T(8,128)S(1)}, u32[]{:S(2)}, u32[]{:S(2)}) collective-permute-start(f32[32,512]{1,0:T(8,128)S(1)} %get-tuple-element.60), channel_id=1, source_target_pairs={{0,4},{2,6},{4,0},{6,2},{1,5},{3,7},{5,1},{7,3},{8,12},{10,14},{12... | collective-permute-start | bytes 196616 | tf_op jit(solution)/shard_map/ppermute | solution.py:53
  62.4 5.5 %collective-permute-start.6 = (f32[32,512]{1,0:T(8,128)S(1)}, f32[32,512]{1,0:T(8,128)S(1)}, u32[]{:S(2)}, u32[]{:S(2)}) collective-permute-start(f32[32,512]{1,0:T(8,128)S(1)} %get-tuple-element.62), channel_id=1, source_target_pairs={{0,2},{2,4},{4,6},{6,0},{1,3},{3,5},{5,7},{7,1},{8,10},{10,12},{12... | collective-permute-start | bytes 196616 | tf_op jit(solution)/shard_map/ppermute | solution.py:53
  64.4 4.3 %collective-permute-start.7 = (f32[32,512]{1,0:T(8,128)S(1)}, f32[32,512]{1,0:T(8,128)S(1)}, u32[]{:S(2)}, u32[]{:S(2)}) collective-permute-start(f32[32,512]{1,0:T(8,128)S(1)} %get-tuple-element.61), channel_id=1, source_target_pairs={{0,6},{2,0},{4,2},{6,4},{1,7},{3,1},{5,3},{7,5},{8,14},{10,8},{12,... | collective-permute-start | bytes 196616 | tf_op jit(solution)/shard_map/ppermute | solution.py:53
  69.0 4.4 %collective-permute-start.8 = (f32[32,512]{1,0:T(8,128)S(1)}, f32[32,512]{1,0:T(8,128)S(1)}, u32[]{:S(2)}, u32[]{:S(2)}) collective-permute-start(f32[32,512]{1,0:T(8,128)S(1)} %fusion.99), channel_id=1, source_target_pairs={{0,64},{8,72},{16,80},{24,88},{32,96},{40,104},{48,112},{56,120},{... | collective-permute-start | bytes 196616 | tf_op jit(solution)/shard_map/ppermute | solution.py:21
  74.6 19.0 %all-to-all-start.2 = ((f32[8,32,512]{2,1,0:T(8,128)}), f32[8,32,512]{2,1,0:T(8,128)S(1)}, u32[]{:S(2)}, u32[]{:S(2)}) async-start(f32[8,32,512]{2,1,0:T(8,128)} %broadcast_in_dim.19), calls=%async_computation.2 | async-start | bytes 1048576 | tf_op jit(solution)/shard_map/all_to_all | solution.py:33
  93.5 10.4 %collective-permute-start.9 = (f32[256,512]{1,0:T(8,128)S(1)}, f32[256,512]{1,0:T(8,128)S(1)}, u32[]{:S(2)}, u32[]{:S(2)}) collective-permute-start(f32[256,512]{1,0:T(8,128)S(1)} %bitcast.217), channel_id=1, source_target_pairs={{0,64},{8,72},{16,80},{24,88},{32,96},{40,104},{48,112},{56,120},{... | collective-permute-start | bytes 1572872 | tf_op jit(solution)/shard_map/ppermute | solution.py:21
  104.6 29.7 %copy-start.1 = (f32[2,16,1,1,32,256]{5,4,3,2,1,0:T(8,128)S(1)}, f32[2,16,1,1,32,256]{5,4,3,2,1,0:T(8,128)}, u32[]{:S(2)}) copy-start(f32[2,16,1,1,32,256]{5,4,3,2,1,0:T(8,128)} %param.15) | copy-start | bytes 3145732
  104.7 29.7 %copy-start.2 = (f32[2,16,1,1,32,256]{5,4,3,2,1,0:T(8,128)S(1)}, f32[2,16,1,1,32,256]{5,4,3,2,1,0:T(8,128)}, u32[]{:S(2)}) copy-start(f32[2,16,1,1,32,256]{5,4,3,2,1,0:T(8,128)} %param.13) | copy-start | bytes 3145732
  104.7 1.6 collective-permute-start.10
  106.4 5.9 %collective-permute-start.11 = (f32[32,512]{1,0:T(8,128)S(1)}, f32[32,512]{1,0:T(8,128)S(1)}, u32[]{:S(2)}, u32[]{:S(2)}) collective-permute-start(f32[32,512]{1,0:T(8,128)S(1)} %get-tuple-element.57), channel_id=1, source_target_pairs={{0,4},{2,6},{4,0},{6,2},{1,5},{3,7},{5,1},{7,3},{8,12},{10,14},{12... | collective-permute-start | bytes 196616 | tf_op jit(solution)/shard_map/ppermute | solution.py:53
  108.8 5.5 %collective-permute-start.12 = (f32[32,512]{1,0:T(8,128)S(1)}, f32[32,512]{1,0:T(8,128)S(1)}, u32[]{:S(2)}, u32[]{:S(2)}) collective-permute-start(f32[32,512]{1,0:T(8,128)S(1)} %get-tuple-element.59), channel_id=1, source_target_pairs={{0,2},{2,4},{4,6},{6,0},{1,3},{3,5},{5,7},{7,1},{8,10},{10,12},{12... | collective-permute-start | bytes 196616 | tf_op jit(solution)/shard_map/ppermute | solution.py:53
  109.7 4.6 %collective-permute-start.13 = (f32[32,512]{1,0:T(8,128)S(1)}, f32[32,512]{1,0:T(8,128)S(1)}, u32[]{:S(2)}, u32[]{:S(2)}) collective-permute-start(f32[32,512]{1,0:T(8,128)S(1)} %get-tuple-element.58), channel_id=1, source_target_pairs={{0,6},{2,0},{4,2},{6,4},{1,7},{3,1},{5,3},{7,5},{8,14},{10,8},{12,... | collective-permute-start | bytes 196616 | tf_op jit(solution)/shard_map/ppermute | solution.py:53
  133.8 10.5 %collective-permute-start.14 = (f32[256,512]{1,0:T(8,128)S(1)}, f32[256,512]{1,0:T(8,128)S(1)}, u32[]{:S(2)}, u32[]{:S(2)}) collective-permute-start(f32[256,512]{1,0:T(8,128)S(1)} %bitcast.222), channel_id=1, source_target_pairs={{0,64},{8,72},{16,80},{24,88},{32,96},{40,104},{48,112},{56,120},{... | collective-permute-start | bytes 1572872 | tf_op jit(solution)/shard_map/ppermute | solution.py:21
  145.0 1.6 collective-permute-start.15
  146.7 7.1 %collective-permute-start.16 = (f32[32,512]{1,0:T(8,128)S(1)}, f32[32,512]{1,0:T(8,128)S(1)}, u32[]{:S(2)}, u32[]{:S(2)}) collective-permute-start(f32[32,512]{1,0:T(8,128)S(1)} %get-tuple-element.54), channel_id=1, source_target_pairs={{0,4},{2,6},{4,0},{6,2},{1,5},{3,7},{5,1},{7,3},{8,12},{10,14},{12... | collective-permute-start | bytes 196616 | tf_op jit(solution)/shard_map/ppermute | solution.py:53
  149.0 7.0 %collective-permute-start.17 = (f32[32,512]{1,0:T(8,128)S(1)}, f32[32,512]{1,0:T(8,128)S(1)}, u32[]{:S(2)}, u32[]{:S(2)}) collective-permute-start(f32[32,512]{1,0:T(8,128)S(1)} %get-tuple-element.56), channel_id=1, source_target_pairs={{0,2},{2,4},{4,6},{6,0},{1,3},{3,5},{5,7},{7,1},{8,10},{10,12},{12... | collective-permute-start | bytes 196616 | tf_op jit(solution)/shard_map/ppermute | solution.py:53
  151.2 4.8 %collective-permute-start.18 = (f32[32,512]{1,0:T(8,128)S(1)}, f32[32,512]{1,0:T(8,128)S(1)}, u32[]{:S(2)}, u32[]{:S(2)}) collective-permute-start(f32[32,512]{1,0:T(8,128)S(1)} %get-tuple-element.55), channel_id=1, source_target_pairs={{0,6},{2,0},{4,2},{6,4},{1,7},{3,1},{5,3},{7,5},{8,14},{10,8},{12,... | collective-permute-start | bytes 196616 | tf_op jit(solution)/shard_map/ppermute | solution.py:53
  156.3 5.9 %collective-permute-start.19 = (f32[32,512]{1,0:T(8,128)S(1)}, f32[32,512]{1,0:T(8,128)S(1)}, u32[]{:S(2)}, u32[]{:S(2)}) collective-permute-start(f32[32,512]{1,0:T(8,128)S(1)} %fusion.97), channel_id=1, source_target_pairs={{0,128},{8,136},{16,144},{24,152},{32,160},{40,168},{48,176},{56,1... | collective-permute-start | bytes 196616 | tf_op jit(solution)/shard_map/ppermute | solution.py:21
  163.4 19.2 %all-to-all-start.4 = ((f32[8,32,512]{2,1,0:T(8,128)}), f32[8,32,512]{2,1,0:T(8,128)S(1)}, u32[]{:S(2)}, u32[]{:S(2)}) async-start(f32[8,32,512]{2,1,0:T(8,128)} %broadcast_in_dim.21), calls=%async_computation.4 | async-start | bytes 1048576 | tf_op jit(solution)/shard_map/all_to_all | solution.py:33
  182.6 16.4 %collective-permute-start.20 = (f32[256,512]{1,0:T(8,128)S(1)}, f32[256,512]{1,0:T(8,128)S(1)}, u32[]{:S(2)}, u32[]{:S(2)}) collective-permute-start(f32[256,512]{1,0:T(8,128)S(1)} %bitcast.212), channel_id=1, source_target_pairs={{0,128},{8,136},{16,144},{24,152},{32,160},{40,168},{48,176},{56,1... | collective-permute-start | bytes 1572872 | tf_op jit(solution)/shard_map/ppermute | solution.py:26
  186.5 19.4 %collective-permute-start.22 = (f32[256,512]{1,0:T(8,128)S(1)}, f32[256,512]{1,0:T(8,128)S(1)}, u32[]{:S(2)}, u32[]{:S(2)}) collective-permute-start(f32[256,512]{1,0:T(8,128)S(1)} %bitcast.213), channel_id=1, source_target_pairs={{0,64},{8,72},{16,80},{24,88},{32,96},{40,104},{48,112},{56,120},{... | collective-permute-start | bytes 1572872 | tf_op jit(solution)/shard_map/ppermute | solution.py:26
  186.7 19.4 %collective-permute-start.21 = (f32[256,512]{1,0:T(8,128)S(1)}, f32[256,512]{1,0:T(8,128)S(1)}, u32[]{:S(2)}, u32[]{:S(2)}) collective-permute-start(f32[256,512]{1,0:T(8,128)S(1)} %bitcast.215), channel_id=1, source_target_pairs={{0,192},{8,200},{16,208},{24,216},{32,224},{40,232},{48,240},{56,2... | collective-permute-start | bytes 1572872 | tf_op jit(solution)/shard_map/ppermute | solution.py:26
  208.1 1.6 collective-permute-start.23
  209.8 7.3 %collective-permute-start.24 = (f32[32,512]{1,0:T(8,128)S(1)}, f32[32,512]{1,0:T(8,128)S(1)}, u32[]{:S(2)}, u32[]{:S(2)}) collective-permute-start(f32[32,512]{1,0:T(8,128)S(1)} %get-tuple-element.51), channel_id=1, source_target_pairs={{0,4},{2,6},{4,0},{6,2},{1,5},{3,7},{5,1},{7,3},{8,12},{10,14},{12... | collective-permute-start | bytes 196616 | tf_op jit(solution)/shard_map/ppermute | solution.py:53
  212.6 6.7 %collective-permute-start.25 = (f32[32,512]{1,0:T(8,128)S(1)}, f32[32,512]{1,0:T(8,128)S(1)}, u32[]{:S(2)}, u32[]{:S(2)}) collective-permute-start(f32[32,512]{1,0:T(8,128)S(1)} %get-tuple-element.53), channel_id=1, source_target_pairs={{0,2},{2,4},{4,6},{6,0},{1,3},{3,5},{5,7},{7,1},{8,10},{10,12},{12... | collective-permute-start | bytes 196616 | tf_op jit(solution)/shard_map/ppermute | solution.py:53
  214.5 4.8 %collective-permute-start.26 = (f32[32,512]{1,0:T(8,128)S(1)}, f32[32,512]{1,0:T(8,128)S(1)}, u32[]{:S(2)}, u32[]{:S(2)}) collective-permute-start(f32[32,512]{1,0:T(8,128)S(1)} %get-tuple-element.52), channel_id=1, source_target_pairs={{0,6},{2,0},{4,2},{6,4},{1,7},{3,1},{5,3},{7,5},{8,14},{10,8},{12,... | collective-permute-start | bytes 196616 | tf_op jit(solution)/shard_map/ppermute | solution.py:53
  219.3 5.9 %collective-permute-start.27 = (f32[32,512]{1,0:T(8,128)S(1)}, f32[32,512]{1,0:T(8,128)S(1)}, u32[]{:S(2)}, u32[]{:S(2)}) collective-permute-start(f32[32,512]{1,0:T(8,128)S(1)} %fusion.83), channel_id=1, source_target_pairs={{0,128},{8,136},{16,144},{24,152},{32,160},{40,168},{48,176},{56,1... | collective-permute-start | bytes 196616 | tf_op jit(solution)/shard_map/ppermute | solution.py:21
  243.9 10.2 %collective-permute-start.28 = (f32[256,512]{1,0:T(8,128)S(1)}, f32[256,512]{1,0:T(8,128)S(1)}, u32[]{:S(2)}, u32[]{:S(2)}) collective-permute-start(f32[256,512]{1,0:T(8,128)S(1)} %bitcast.225), channel_id=1, source_target_pairs={{0,64},{8,72},{16,80},{24,88},{32,96},{40,104},{48,112},{56,120},{... | collective-permute-start | bytes 1572872 | tf_op jit(solution)/shard_map/ppermute | solution.py:21
  254.8 1.6 collective-permute-start.29
  256.5 32.6 %copy-start.5 = (f32[2,8,1,1,32,256]{5,4,3,2,1,0:T(8,128)S(1)}, f32[2,8,1,1,32,256]{5,4,3,2,1,0:T(8,128)}, u32[]{:S(2)}) copy-start(f32[2,8,1,1,32,256]{5,4,3,2,1,0:T(8,128)} %param.16) | copy-start | bytes 1572868
  256.5 6.3 %collective-permute-start.30 = (f32[32,512]{1,0:T(8,128)S(1)}, f32[32,512]{1,0:T(8,128)S(1)}, u32[]{:S(2)}, u32[]{:S(2)}) collective-permute-start(f32[32,512]{1,0:T(8,128)S(1)} %get-tuple-element.48), channel_id=1, source_target_pairs={{0,4},{2,6},{4,0},{6,2},{1,5},{3,7},{5,1},{7,3},{8,12},{10,14},{12... | collective-permute-start | bytes 196616 | tf_op jit(solution)/shard_map/ppermute | solution.py:53
  258.7 6.4 %collective-permute-start.31 = (f32[32,512]{1,0:T(8,128)S(1)}, f32[32,512]{1,0:T(8,128)S(1)}, u32[]{:S(2)}, u32[]{:S(2)}) collective-permute-start(f32[32,512]{1,0:T(8,128)S(1)} %get-tuple-element.50), channel_id=1, source_target_pairs={{0,2},{2,4},{4,6},{6,0},{1,3},{3,5},{5,7},{7,1},{8,10},{10,12},{12... | collective-permute-start | bytes 196616 | tf_op jit(solution)/shard_map/ppermute | solution.py:53
  260.3 4.8 %collective-permute-start.32 = (f32[32,512]{1,0:T(8,128)S(1)}, f32[32,512]{1,0:T(8,128)S(1)}, u32[]{:S(2)}, u32[]{:S(2)}) collective-permute-start(f32[32,512]{1,0:T(8,128)S(1)} %get-tuple-element.49), channel_id=1, source_target_pairs={{0,6},{2,0},{4,2},{6,4},{1,7},{3,1},{5,3},{7,5},{8,14},{10,8},{12,... | collective-permute-start | bytes 196616 | tf_op jit(solution)/shard_map/ppermute | solution.py:53
  265.1 4.4 %collective-permute-start.33 = (f32[32,512]{1,0:T(8,128)S(1)}, f32[32,512]{1,0:T(8,128)S(1)}, u32[]{:S(2)}, u32[]{:S(2)}) collective-permute-start(f32[32,512]{1,0:T(8,128)S(1)} %fusion.81), channel_id=1, source_target_pairs={{0,64},{8,72},{16,80},{24,88},{32,96},{40,104},{48,112},{56,120},{... | collective-permute-start | bytes 196616 | tf_op jit(solution)/shard_map/ppermute | solution.py:21
  289.7 1.6 collective-permute-start.34
  291.4 6.4 %collective-permute-start.35 = (f32[32,512]{1,0:T(8,128)S(1)}, f32[32,512]{1,0:T(8,128)S(1)}, u32[]{:S(2)}, u32[]{:S(2)}) collective-permute-start(f32[32,512]{1,0:T(8,128)S(1)} %get-tuple-element.45), channel_id=1, source_target_pairs={{0,4},{2,6},{4,0},{6,2},{1,5},{3,7},{5,1},{7,3},{8,12},{10,14},{12... | collective-permute-start | bytes 196616 | tf_op jit(solution)/shard_map/ppermute | solution.py:53
  294.5 5.5 %collective-permute-start.36 = (f32[32,512]{1,0:T(8,128)S(1)}, f32[32,512]{1,0:T(8,128)S(1)}, u32[]{:S(2)}, u32[]{:S(2)}) collective-permute-start(f32[32,512]{1,0:T(8,128)S(1)} %get-tuple-element.47), channel_id=1, source_target_pairs={{0,2},{2,4},{4,6},{6,0},{1,3},{3,5},{5,7},{7,1},{8,10},{10,12},{12... | collective-permute-start | bytes 196616 | tf_op jit(solution)/shard_map/ppermute | solution.py:53
  295.3 4.7 %collective-permute-start.37 = (f32[32,512]{1,0:T(8,128)S(1)}, f32[32,512]{1,0:T(8,128)S(1)}, u32[]{:S(2)}, u32[]{:S(2)}) collective-permute-start(f32[32,512]{1,0:T(8,128)S(1)} %get-tuple-element.46), channel_id=1, source_target_pairs={{0,6},{2,0},{4,2},{6,4},{1,7},{3,1},{5,3},{7,5},{8,14},{10,8},{12,... | collective-permute-start | bytes 196616 | tf_op jit(solution)/shard_map/ppermute | solution.py:53
